TPU v7x, 32 devices: a whole 2x2x4 slice. The times are simulated.
32 devices in a mesh: groups: 2 (over y), charge: 8 (over z, core), split: 2 (over x).
Axes of the slice: x: 2, y: 2, z: 4, core: 2. Of those that a mesh axis runs over, the one named last changes fastest.
Arguments:
- left_env: bfloat16 [16, 1024, 1024], P(('groups', 'charge'), 'split'), parts along dimension 0, may hold values from -6 to 6
- site_tensor: bfloat16 [16, 4, 1024, 1024], P(('groups', 'charge'), None, None, 'split'), parts along dimension 0, may hold values from -0.1875 to 0.1875
- left_sizes: int32 [16], P(('groups', 'charge')), parts along dimension 0, may hold values from 1 to 1024, 4096 in all
- right_sizes: int32 [16], P('groups'), parts along dimension 0, may hold values from 1 to 1024, 4096 in all
- targets: int32 [16, 4], P(('groups', 'charge')), parts along dimension 0, may hold values from 0 to 7, all different within a row
Outputs:
- new_env: float32 [16, 1024, 1024], P('groups', 'charge', 'split'), parts along dimension 0
There are 2 independent parts, one for each index of `groups`. A program takes and returns all parts, laid end to end along the dimension named above; each array names one. Nothing has to cross between parts.
Inputs may be any that keep to these rules, and one draw needn't show every extreme that they name: `targets`: the 4 entries of one row are distinct, and every right-bond sector is reached by some row.
All inputs are finite; a program needn't handle non-finite values. No bound on the sum of `left_sizes` on one device may be relied on, other than what follows from the above.
Results may differ from a plain program's by a relative error of at most 0.015.
Values may be sent and summed in bfloat16 or wider, within the bound.
A program may use at most 64 MiB of HBM per device.

v0:
```python
import functools

import jax
import jax.numpy as jnp
from jax import lax
from jax.experimental import pallas as pl
from jax.experimental.pallas import tpu as pltpu
from jax.sharding import PartitionSpec as P

MESH = pl.DeviceIdType.MESH
LADDER = ((8, 8, 6, 3), (8, 8, 6, 4), (8, 8, 6, 6), (8, 8, 8, 8))


def gathered_body(left_env, site_tensor, left_sizes, right_sizes, targets):
    states = site_tensor.shape[1]
    span = site_tensor.shape[2]
    width = site_tensor.shape[3]
    sectors = right_sizes.shape[0]
    column_base = lax.axis_index("split") * width
    row_ids = lax.broadcasted_iota(jnp.int32, (1, span, 1), 1)
    column_ids = lax.broadcasted_iota(jnp.int32, (1, 1, width), 2) + column_base
    slot_ids = lax.broadcasted_iota(jnp.int32, (states, sectors), 1)
    route = targets[0][:, None] == slot_ids
    live_cols = jnp.sum(jnp.where(route, right_sizes[None, :], 0), axis=1)
    keep = (row_ids < left_sizes[0]) & (column_ids < live_cols[:, None, None])
    masked = jnp.where(keep, site_tensor[0], jnp.zeros((), jnp.bfloat16))[None]
    product = jnp.einsum(
        "ik,skj->sij",
        lax.all_gather(left_env, "split", axis=1, tiled=True)[0],
        masked[0],
        preferred_element_type=jnp.float32,
    ).astype(jnp.bfloat16)
    terms = jnp.einsum(
        "ski,skj->sij",
        lax.all_gather(masked, "split", axis=3, tiled=True)[0],
        product,
        preferred_element_type=jnp.float32,
    ).astype(jnp.bfloat16)
    placed = jnp.einsum(
        "st,sij->tij", route.astype(jnp.bfloat16), terms, preferred_element_type=jnp.float32
    ).astype(jnp.bfloat16)
    return lax.psum_scatter(placed, "charge", scatter_dimension=1, tiled=True).astype(jnp.float32)


def agree(targets_ref, left_ref, right_ref, l_ref, m_ref, inv_ref, meta_ref, pick_ref, lf, ms,
          info, got, seen, site, send, recv, sem, lsend, lrecv, lown, mown):
    g = lax.axis_index("groups")
    me = lax.axis_index("charge")
    h = lax.axis_index("split")
    devices, sectors = inv_ref.shape[0] // 2, right_ref.shape[0]
    others = got.shape[0]
    states = targets_ref.shape[1]
    mine = g * devices + me

    barrier = pltpu.get_barrier_semaphore()

    def place(i):
        n = lax.rem(mine + i, others)
        return {"groups": n // devices, "charge": lax.rem(n, devices)}

    def greet(i, c):
        pl.semaphore_signal(barrier, inc=1, device_id=place(i), device_id_type=MESH)
        return c

    lax.fori_loop(1, others, greet, 0)
    pl.semaphore_signal(barrier, inc=1, device_id={"split": 1 - h}, device_id_type=MESH)

    span, width = ms.shape[1], ms.shape[2]
    half_rows = pl.ds(pl.multiple_of(h * width, width), width)
    m_own = pltpu.make_async_copy(m_ref, site, mown)
    m_own.start()
    l_own = pltpu.make_async_copy(l_ref, lf.at[half_rows], lown)
    l_own.start()
    to = [targets_ref[0, j] for j in range(states)]
    size = [right_ref[t] for t in to]
    rank = []
    for j in range(states):
        ahead = jnp.int32(0)
        for k in range(states):
            if k != j:
                first = size[k] >= size[j] if k < j else size[k] > size[j]
                ahead = ahead + jnp.where(first, 1, 0)
        rank.append(ahead)
    lane = lax.broadcasted_iota(jnp.int32, info.shape, 1)
    packed = jnp.zeros(info.shape, jnp.int32)
    for slot in range(states):
        state, live, target = jnp.int32(0), jnp.int32(0), jnp.int32(0)
        for j in range(states):
            here = rank[j] == slot
            state = jnp.where(here, j, state)
            live = jnp.where(here, size[j], live)
            target = jnp.where(here, to[j], target)
        meta_ref[slot] = state
        meta_ref[states + slot] = live
        packed = jnp.where(lane == slot, target, packed)
        packed = jnp.where(lane == states + slot, live, packed)
    meta_ref[2 * states] = left_ref[0]
    for r in range(sectors):
        meta_ref[2 * states + 1 + r] = right_ref[r]
    info[...] = packed
    got[mine] = packed
    pl.semaphore_wait(barrier, others)
    l_copy = pltpu.make_async_remote_copy(
        src_ref=l_ref, dst_ref=lf.at[half_rows], send_sem=lsend, recv_sem=lrecv,
        device_id={"split": 1 - h}, device_id_type=MESH)
    l_copy.start()

    def copy(i):
        return pltpu.make_async_remote_copy(
            src_ref=info, dst_ref=got.at[mine], send_sem=send.at[i], recv_sem=recv.at[mine],
            device_id=place(i), device_id_type=MESH)

    def start(i, c):
        copy(i).start()
        return c

    def finish(i, c):
        n = lax.rem(mine + i, others)
        copy(i).wait_send()
        pltpu.make_async_remote_copy(
            src_ref=info, dst_ref=got.at[n], send_sem=send.at[i], recv_sem=recv.at[n],
            device_id=place(i), device_id_type=MESH).wait_recv()
        return c

    lax.fori_loop(1, others, start, 0)
    m_own.wait()

    def mask(j, c):
        state, live, deep = meta_ref[j], meta_ref[states + j], meta_ref[2 * states]

        def tile(i, c):
            part = pl.ds(pl.multiple_of(i * 128, 128), 128)
            row_ids = lax.broadcasted_iota(jnp.int32, (128, width), 0) + i * 128
            col_ids = lax.broadcasted_iota(jnp.int32, (128, width), 1) + h * width
            keep = (row_ids < deep) & (col_ids < live)
            ms[j, part] = jnp.where(keep, site[state, part].astype(jnp.float32), 0.0).astype(jnp.bfloat16)
            return c

        return lax.fori_loop(0, span // 128, tile, c)

    lax.fori_loop(0, states, mask, 0)
    lax.fori_loop(1, others, finish, 0)
    local = pltpu.make_async_copy(got, seen, sem)
    local.start()
    local.wait()

    half = devices // 2
    relayed = (h == 0) & (me < half)
    wants, passes = [], []
    for r in range(sectors):
        wants.append(right_ref[r] > jnp.maximum(me * (span // devices), h * width))
        passes.append(right_ref[r] > (me - half) * (span // devices))

    def route(q, c):
        reached = [seen[g * devices + q, 0, j] for j in range(states)]
        for r in range(sectors):
            slot = jnp.int32(states)
            for j in range(states):
                slot = jnp.where(reached[j] == r, j, slot)
            direct = wants[r] & jnp.logical_not(relayed & (q >= half))
            inv_ref[q, r] = jnp.where(direct, slot, states)
            inv_ref[devices + q, r] = jnp.where(passes[r], slot, states)
        return c

    lax.fori_loop(0, devices, route, 0)

    def widest(n, most):
        return tuple(jnp.maximum(m, seen[n, 0, states + j]) for j, m in enumerate(most))

    most = lax.fori_loop(0, others, widest, (jnp.int32(0),) * states)
    pick = jnp.int32(len(LADDER) - 1)
    for at in range(len(LADDER) - 2, -1, -1):
        fits = most[0] <= LADDER[at][0] * 128
        for j in range(1, states):
            fits = fits & (most[j] <= LADDER[at][j] * 128)
        pick = jnp.where(fits, at, pick)
    pick_ref[0] = pick
    l_own.wait()
    l_copy.wait()


def kernel(caps, inv_ref, meta_ref, lf, ms, o_ref, mr, pb, tb, zr, ag, up, down, px, xb,
           xsend, xrecv, msend, mrecv, zsend, zrecv, usend, urecv, dsend, drecv):
    me = lax.axis_index("charge")
    h = lax.axis_index("split")
    devices, empty, rows, width = zr.shape[0], zr.shape[1] - 1, zr.shape[2], zr.shape[3]
    states, span = ms.shape[0], ms.shape[1]
    half = devices // 2
    wide = mr.shape[0]
    f32, bf16 = jnp.float32, jnp.bfloat16

    barrier = pltpu.get_barrier_semaphore()
    pl.semaphore_signal(barrier, inc=1, device_id={"split": 1 - h}, device_id_type=MESH)

    def greet(i, c):
        pl.semaphore_signal(barrier, inc=1, device_id={"charge": lax.rem(me + i, devices)}, device_id_type=MESH)
        return c

    lax.fori_loop(1, devices, greet, 0)
    pl.semaphore_wait(barrier, devices)

    def to_other(src, dst, send, recv):
        return pltpu.make_async_remote_copy(
            src_ref=src, dst_ref=dst, send_sem=send, recv_sem=recv,
            device_id={"split": 1 - h}, device_id_type=MESH)

    m_copies = [to_other(ms.at[j], mr.at[j], msend.at[j], mrecv.at[j]) for j in range(wide)]

    slim = [half < c <= half + 256 // rows for c in caps]
    thin = px.shape[1]

    def slim_copy(j):
        return to_other(ms.at[j, :, pl.ds(0, thin)], mr.at[j, :, pl.ds(0, thin)], msend.at[j], mrecv.at[j])

    def back_copy(j):
        return to_other(xb.at[j], tb.at[j, pl.ds(0, width), pl.ds(0, thin)], xsend.at[j], xrecv.at[j])

    def start_m(j):
        if slim[j]:
            pl.when(h == 1)(lambda: slim_copy(j).start())
        else:
            m_copies[j].start()

    start_m(0)

    def product(j):
        def tile(i, c):
            part = pl.ds(pl.multiple_of(i * 256, 256), 256)
            pb[j, part] = jnp.dot(lf[part], ms[j], preferred_element_type=f32).astype(bf16)
            return c

        lax.fori_loop(0, span // 256, tile, 0)

    def term(j, columns, which):
        for i in range(width // 256):
            part = pl.ds(pl.multiple_of(which * width + i * 256, 256), 256)
            tb[j, part] = lax.dot_general(
                columns[j, :, i * 256:(i + 1) * 256], pb[j], (((0,), (0,)), ((), ())),
                preferred_element_type=f32).astype(bf16)

    def live_width(j, side):
        return (caps[j] - half if side else min(caps[j], half)) * rows

    def chunk(j, d, source, side):
        part = pl.ds(pl.multiple_of(d * rows, rows), rows)
        columns = pl.ds(0, live_width(j, side))
        return pltpu.make_async_remote_copy(
            src_ref=tb.at[j, part, columns], dst_ref=zr.at[source, j, :, columns],
            send_sem=zsend.at[j, d], recv_sem=zrecv.at[source, j],
            device_id={"charge": d}, device_id_type=MESH)

    def scatter(j, side, lower):
        first = 0 if lower else half
        count = min(caps[j], half) if lower else caps[j] - half

        def one(i, c):
            d = first + lax.rem(me + 1 + i, count)

            @pl.when(d != me)
            def _():
                chunk(j, d, me, side).start()

            @pl.when(d == me)
            def _():
                zr[me, j] = tb[j, pl.ds(pl.multiple_of(d * rows, rows), rows)]

            return c

        lax.fori_loop(0, count, one, 0)

    upper, lower = (h == 0) & (me >= half), (h == 0) & (me < half)
    sectors = o_ref.shape[0]

    def lift(j, d, source):
        part = pl.ds(pl.multiple_of(d * rows, rows), rows)
        columns = pl.ds(0, live_width(j, 0))
        return pltpu.make_async_remote_copy(
            src_ref=tb.at[j, part, columns], dst_ref=ag.at[source, j, :, columns],
            send_sem=usend.at[j, d], recv_sem=urecv.at[source, j],
            device_id={"charge": half + d}, device_id_type=MESH)

    def collect(j):
        count = min(caps[j], half)

        def one(i, c):
            d = lax.rem(me + 1 + i, count)

            @pl.when(half + d != me)
            def _():
                lift(j, d, me - half).start()

            @pl.when(half + d == me)
            def _():
                ag[me - half, j] = tb[j, pl.ds(pl.multiple_of(d * rows, rows), rows)]

            return c

        lax.fori_loop(0, count, one, 0)

    def hand_down(r):
        return pltpu.make_async_remote_copy(
            src_ref=up.at[r], dst_ref=down.at[r], send_sem=dsend.at[r], recv_sem=drecv.at[r],
            device_id={"charge": me - half}, device_id_type=MESH)

    def relay():
        own = me - half

        def arrive(i, c):
            source = lax.rem(own + i, half)
            for j in range(states):
                pl.when(own < caps[j])(lambda j=j: lift(j, source, source).wait_recv())
            return c

        lax.fori_loop(1, half, arrive, 0)

        def send(r, c):
            total = ag[0, inv_ref[devices + half, r]].astype(f32)
            for source in range(1, half):
                total = total + ag[source, inv_ref[devices + half + source, r]].astype(f32)
            up[r] = total.astype(bf16)
            hand_down(r).start()
            return c

        lax.fori_loop(0, sectors, send, 0)

    def relay_sent():
        def left(i, c):
            d = lax.rem(me - half + i, half)
            for j in range(states):
                pl.when(d < caps[j])(lambda j=j: lift(j, d, d).wait_send())
            return c

        lax.fori_loop(1, half, left, 0)

        def gone(r, c):
            hand_down(r).wait_send()
            return c

        lax.fori_loop(0, sectors, gone, 0)

    def relay_received():
        def got(r, c):
            pltpu.make_async_remote_copy(
                src_ref=up.at[r], dst_ref=down.at[r], send_sem=dsend.at[r], recv_sem=drecv.at[r],
                device_id={"charge": me + half}, device_id_type=MESH).wait_recv()
            return c

        lax.fori_loop(0, sectors, got, 0)

    def near(j):
        product(j)
        term(j, ms, h)
        pl.when(lower)(functools.partial(scatter, j, 0, True))
        pl.when(upper)(functools.partial(collect, j))
        if caps[j] > half:
            pl.when(h == 1)(functools.partial(scatter, j, 1, False))

    for j in range(states):
        if j < wide:
            near(j)
        else:
            pl.when(h == 0)(functools.partial(near, j))
        if j == 1:
            start_m(1)
    zr[:, empty] = jnp.zeros((devices, rows, width), bf16)
    ag[:, empty] = jnp.zeros((half, rows, width), bf16)

    @pl.when(jnp.logical_not(lower))
    def _():
        down[...] = jnp.zeros(down.shape, bf16)

    def far_slim(j):
        slim_copy(j).wait_recv()

        def tile(i, c):
            part = pl.ds(pl.multiple_of(i * 256, 256), 256)
            px[part] = jnp.dot(lf[part], mr[j, :, 0:thin], preferred_element_type=f32).astype(bf16)
            return c

        lax.fori_loop(0, span // 256, tile, 0)
        for i in range(width // 256):
            xb[j, i * 256:(i + 1) * 256] = lax.dot_general(
                ms[j, :, i * 256:(i + 1) * 256], px[...], (((0,), (0,)), ((), ())),
                preferred_element_type=f32).astype(bf16)
        back_copy(j).start()
        tb[j, width:width + thin] = lax.dot_general(
            mr[j, :, 0:thin], pb[j], (((0,), (0,)), ((), ())), preferred_element_type=f32).astype(bf16)
        scatter(j, 0, False)

    def far_back(j):
        back_copy(j).wait_recv()
        scatter(j, 1, True)

    for j in range(wide):
        if slim[j]:
            if j + 2 < wide:
                start_m(j + 2)
            pl.when(h == 0)(functools.partial(far_slim, j))
            pl.when(h == 1)(functools.partial(far_back, j))
            continue
        m_copies[j].wait()
        if j + 2 < wide:
            start_m(j + 2)
        term(j, mr, 1 - h)
        pl.when(h == 0)(functools.partial(scatter, j, 0, False))
        pl.when(h == 1)(functools.partial(scatter, j, 1, True))
        if j == 0:
            pl.when(upper)(relay)
    for j in range(wide):
        if slim[j]:
            pl.when(h == 1)(lambda j=j: slim_copy(j).wait_send())
            pl.when(h == 0)(lambda j=j: back_copy(j).wait_send())

    def settle(i, c):
        other = lax.rem(me + i, devices)
        for j in range(states):
            for side in range(2 if j < wide else 1):
                here, there = (h == side) & (me < caps[j]), (h == side) & (other < caps[j])
                if side == 0:
                    here = here & ((me >= half) | (other < half))
                    there = there & ((me < half) | (other >= half))
                pl.when(here)(lambda j=j, side=side: chunk(j, me, other, side).wait_recv())
                pl.when(there)(lambda j=j, side=side: chunk(j, other, me, side).wait_send())
        return c

    lax.fori_loop(1, devices, settle, 0)
    pl.when(upper)(relay_sent)
    pl.when(lower)(relay_received)

    def add(r, c):
        total = down[r].astype(f32)
        for source in range(devices):
            total = total + zr[source, inv_ref[source, r]].astype(f32)
        col_ids = lax.broadcasted_iota(jnp.int32, total.shape, 1) + h * width
        o_ref[r] = jnp.where(col_ids < meta_ref[2 * states + 1 + r], total, 0.0)
        return c

    lax.fori_loop(0, sectors, add, 0)


def fused(at, inv, meta, whole, site):
    caps = LADDER[at]
    states, span, width = site.shape
    devices, sectors = inv.shape[0] // 2, inv.shape[1]
    rows = span // devices
    wide = sum(c > devices // 2 for c in caps)
    bf16 = jnp.bfloat16
    dma = pltpu.SemaphoreType.DMA
    return pl.pallas_call(
        functools.partial(kernel, caps),
        out_shape=jax.ShapeDtypeStruct((sectors, rows, width), jnp.float32),
        in_specs=[pl.BlockSpec(memory_space=pltpu.SMEM)] * 2 + [pl.BlockSpec(memory_space=pltpu.VMEM)] * 2,
        out_specs=pl.BlockSpec(memory_space=pltpu.VMEM),
        scratch_shapes=[
            pltpu.VMEM((wide, span, width), bf16),
            pltpu.VMEM((states, span, width), bf16),
            pltpu.VMEM((states, span, width), bf16),
            pltpu.VMEM((devices, states + 1, rows, width), bf16),
            pltpu.VMEM((devices // 2, states + 1, rows, width), bf16),
            pltpu.VMEM((sectors, rows, width), bf16),
            pltpu.VMEM((sectors, rows, width), bf16),
            pltpu.VMEM((span, 256), bf16),
            pltpu.VMEM((wide, width, 256), bf16),
            dma((wide,)), dma((wide,)), dma((wide,)), dma((wide,)),
            dma((states, devices)), dma((devices, states)),
            dma((states, devices // 2)), dma((devices // 2, states)), dma((sectors,)), dma((sectors,)),
        ],
        compiler_params=pltpu.CompilerParams(
            collective_id=1 + at, has_side_effects=True, vmem_limit_bytes=50 * 2**20),
        cost_estimate=pl.CostEstimate(
            flops=4 * states * span * span * width, bytes_accessed=16 * 2**20, transcendentals=0),
    )(inv, meta, whole, site)


def body(groups, devices, left_env, site_tensor, left_sizes, right_sizes, targets):
    states = site_tensor.shape[1]
    sectors = right_sizes.shape[0]
    others = groups * devices
    i32 = jnp.int32
    dma = pltpu.SemaphoreType.DMA
    smem = pl.BlockSpec(memory_space=pltpu.SMEM)
    vmem = pl.BlockSpec(memory_space=pltpu.VMEM)
    inv, meta, pick, whole, masked = pl.pallas_call(
        agree,
        out_shape=[
            jax.ShapeDtypeStruct((2 * devices, sectors), i32),
            jax.ShapeDtypeStruct((2 * states + 1 + sectors,), i32),
            jax.ShapeDtypeStruct((1,), i32),
            jax.ShapeDtypeStruct((site_tensor.shape[2],) * 2, jnp.bfloat16),
            jax.ShapeDtypeStruct(site_tensor.shape[1:], jnp.bfloat16),
        ],
        in_specs=[smem] * 3 + [pl.BlockSpec(memory_space=pltpu.HBM)] * 2,
        out_specs=[smem] * 3 + [vmem] * 2,
        scratch_shapes=[
            pltpu.VMEM((8, 128), i32), pltpu.VMEM((others, 8, 128), i32), pltpu.SMEM((others, 8, 128), i32),
            pltpu.VMEM(site_tensor.shape[1:], jnp.bfloat16),
            dma((others,)), dma((others,)), dma, dma, dma, dma, dma,
        ],
        compiler_params=pltpu.CompilerParams(collective_id=0, has_side_effects=True, vmem_limit_bytes=24 * 2**20),
    )(targets, left_sizes, right_sizes, left_env[0], site_tensor[0])
    branches = [functools.partial(fused, at) for at in range(len(LADDER))]
    return lax.switch(pick[0], branches, inv, meta, whole, masked)


def solution(mesh):
    in_specs = (
        P(("groups", "charge"), "split", None),
        P(("groups", "charge"), None, None, "split"),
        P(("groups", "charge")),
        P("groups"),
        P(("groups", "charge"), None),
    )
    out_specs = P("groups", "charge", "split")
    if mesh.shape["split"] == 2 and mesh.shape["charge"] == 8:
        inner = functools.partial(body, mesh.shape["groups"], mesh.shape["charge"])
    else:
        inner = gathered_body
    return jax.shard_map(inner, mesh=mesh, in_specs=in_specs, out_specs=out_specs, check_vma=False)
```

profile of v0, /device:TPU:2, one launch (start us, length us, event | category | flops | bytes accessed | tf_op | source)
XLA Modules:
  0.0 126.4 jit_solution(3566590651573015133)
XLA Ops:
  0.7 0.0 copy-start
  0.7 2.2 %copy-done = bf16[1,4,1024,512]{3,2,1,0:T(8,128)(2,1)S(1)} copy-done((bf16[1,4,1024,512]{3,2,1,0:T(8,128)(2,1)S(1)}, bf16[1,4,1024,512]{3,2,1,0:T(8,128)(2,1)}, u32[]{:S(2)}) %copy-start) | copy-done | bytes 4194328
  2.8 0.0 copy-start.1
  2.8 1.2 copy-done.1
  4.1 0.0 copy-start.2
  4.1 0.7 copy-done.2
  4.7 0.0 copy-start.3
  4.7 0.7 copy-done.3
  5.4 30.2 %shard_map.59 = (s32[16,8]{1,0:T(8,128)S(1)}, s32[17]{0:T(128)S(1)}, s32[1]{0:T(128)}, bf16[1024,1024]{1,0:T(8,128)(2,1)S(1)}, bf16[4,1024,512]{2,1,0:T(8,128)(2,1)S(1)}) custom-call(s32[1,4]{1,0:T(1,128)S(1)} %copy-done.2, s32[1]{0:T(128)S(6)} %copy.15.left_ref, s32[8]{0:T(128)S(1)} %copy-done.3, bf16[512,1024]{1,0:T(8,128)(2,1)S(1)} %bitcast.4, ...), custom_call_target="tpu_custom_call" | custom-call | tf_op jit(solution)/shard_map/pallas_call | solution.py:483
  36.3 88.7 %conditional.1 = (f32[8,128,512]{2,1,0:T(8,128)S(1)}) conditional(s32[]{:T(128)} %bitcast.2, (s32[16,8]{1,0:T(8,128)S(1)}, s32[17]{0:T(128)S(1)}, bf16[1024,1024]{1,0:T(8,128)(2,1)S(1)}, bf16[4,1024,512]{2,1,0:T(8,128)(2,1)S(1)}) %tuple.17, (s32[16,8]{1,0:T(8,128)S(1)}, s32[17]{0:T(128)S(1)}, ...), branch_computations={%region_0.0_spmd, %region_1.0_spmd, %region_2.0_spmd, %region_3.0_... | conditional | flops 8589934592 | bytes 16777224 | solution.py:502
  36.3 88.5 %branch_0_fun.1 = f32[8,128,512]{2,1,0:T(8,128)S(1)} custom-call(s32[16,8]{1,0:T(8,128)S(1)} %get-tuple-element.40.inv_ref, s32[17]{0:T(128)S(1)} %get-tuple-element.42.meta_ref, bf16[1024,1024]{1,0:T(8,128)(2,1)S(1)} %get-tuple-element.44.lf, bf16[4,1024,512]{2,1,0:T(8,128)(2,1)S(1)} %get-tuple-element.45.ms), custom_call_target="tpu_custom_call" | custom-call | flops 8589934592 | bytes 16777216 | tf_op jit(solution)/shard_map/cond/branch_0_fun/pallas_call | solution.py:449
  125.0 1.3 %copy.16 = f32[8,128,512]{2,1,0:T(8,128)} copy(f32[8,128,512]{2,1,0:T(8,128)S(1)} %get-tuple-element.68) | data formatting | bytes 4194304
Async XLA Ops:
  0.7 2.2 %copy-start = (bf16[1,4,1024,512]{3,2,1,0:T(8,128)(2,1)S(1)}, bf16[1,4,1024,512]{3,2,1,0:T(8,128)(2,1)}, u32[]{:S(2)}) copy-start(bf16[1,4,1024,512]{3,2,1,0:T(8,128)(2,1)} %param.10) | copy-start | bytes 12582916
  2.8 1.2 copy-start.1
  4.1 0.7 copy-start.2
  4.7 0.7 copy-start.3
where the time goes:
time: 127 us; the launch traced here: 126 us
  Pallas kernels  119 us (94%)
  local copies, waits for them, and re-layouts  6.04 us (5%)
  between operations  1.37 us (1%)
    pallas_call x1, Pallas kernels, fused(): pl.pallas_call(functools.partial(kernel, caps), out_shape=jax.ShapeDtypeS...  88.5 us
    pallas_call x1, Pallas kernels, body(): pl.pallas_call(agree, out_shape=[jax.ShapeDtypeStruct((2 * devices, secto...  30.2 us
    unnamed x9, local copies, waits for them, and re-layouts  6.04 us

commit v1 on v0

--- a/solution.py
+++ b/solution.py
@@ -496,7 +496,7 @@
             pltpu.VMEM(site_tensor.shape[1:], jnp.bfloat16),
             dma((others,)), dma((others,)), dma, dma, dma, dma, dma,
         ],
-        compiler_params=pltpu.CompilerParams(collective_id=0, has_side_effects=True, vmem_limit_bytes=24 * 2**20),
+        compiler_params=pltpu.CompilerParams(collective_id=0, has_side_effects=True, vmem_limit_bytes=54 * 2**20),
     )(targets, left_sizes, right_sizes, left_env[0], site_tensor[0])
     branches = [functools.partial(fused, at) for at in range(len(LADDER))]
     return lax.switch(pick[0], branches, inv, meta, whole, masked)

time: 127 us -> 122 us (0.961)
  local copies, waits for them, and re-layouts: 6.04 us -> 1.32 us
    unnamed x9 -> x1, local copies, waits for them, and re-layouts: 6.04 us -> 1.32 us
where the time goes in v1:
time: 122 us
  Pallas kernels  119 us (98%)
  local copies, waits for them, and re-layouts  1.32 us (1%)
  between operations  1.3 us (1%)
    pallas_call x1, Pallas kernels, fused(): pl.pallas_call(functools.partial(kernel, caps), out_shape=jax.ShapeDtypeS...  88.5 us
    pallas_call x1, Pallas kernels, body(): pl.pallas_call(agree, out_shape=[jax.ShapeDtypeStruct((2 * devices, secto...  30.6 us

profile of v1, /device:TPU:2, one launch (start us, length us, event | category | flops | bytes accessed | tf_op | source)
XLA Modules:
  0.0 121.9 jit_solution(10696503599683790261)
XLA Ops:
  0.7 30.6 %shard_map.59 = (s32[16,8]{1,0:T(8,128)S(1)}, s32[17]{0:T(128)S(1)}, s32[1]{0:T(128)}, bf16[1024,1024]{1,0:T(8,128)(2,1)S(1)}, bf16[4,1024,512]{2,1,0:T(8,128)(2,1)S(1)}) custom-call(s32[1,4]{1,0:T(1,128)} %targets_ref.1, s32[1]{0:T(128)S(6)} %copy.15.left_ref, s32[8]{0:T(128)} %right_ref.1, bf16[512,1024]{1,0:T(8,128)(2,1)} %bitcast.4, ...), custom_call_target="tpu_custom_call" | custom-call | tf_op jit(solution)/shard_map/pallas_call | solution.py:483
  31.9 88.7 %conditional.1 = (f32[8,128,512]{2,1,0:T(8,128)S(1)}) conditional(s32[]{:T(128)} %bitcast.2, (s32[16,8]{1,0:T(8,128)S(1)}, s32[17]{0:T(128)S(1)}, bf16[1024,1024]{1,0:T(8,128)(2,1)S(1)}, bf16[4,1024,512]{2,1,0:T(8,128)(2,1)S(1)}) %tuple.17, (s32[16,8]{1,0:T(8,128)S(1)}, s32[17]{0:T(128)S(1)}, ...), branch_computations={%region_0.0_spmd, %region_1.0_spmd, %region_2.0_spmd, %region_3.0_... | conditional | flops 8589934592 | bytes 16777224 | solution.py:502
  31.9 88.5 %branch_0_fun.1 = f32[8,128,512]{2,1,0:T(8,128)S(1)} custom-call(s32[16,8]{1,0:T(8,128)S(1)} %get-tuple-element.40.inv_ref, s32[17]{0:T(128)S(1)} %get-tuple-element.42.meta_ref, bf16[1024,1024]{1,0:T(8,128)(2,1)S(1)} %get-tuple-element.44.lf, bf16[4,1024,512]{2,1,0:T(8,128)(2,1)S(1)} %get-tuple-element.45.ms), custom_call_target="tpu_custom_call" | custom-call | flops 8589934592 | bytes 16777216 | tf_op jit(solution)/shard_map/cond/branch_0_fun/pallas_call | solution.py:449
  120.6 1.3 %copy.16 = f32[8,128,512]{2,1,0:T(8,128)} copy(f32[8,128,512]{2,1,0:T(8,128)S(1)} %get-tuple-element.68) | data formatting | bytes 4194304
